TPU v7x, 32 devices: a whole 2x2x4 slice. The times are simulated.
32 devices in a mesh: grp: 2 (over y), row: 8 (over z, x), col: 2 (over core).
Axes of the slice: x: 2, y: 2, z: 4, core: 2. Of those that a mesh axis runs over, the one named last changes fastest.
Arguments:
- tokens: bfloat16 [128, 256, 180], P(('grp', 'row'), 'col'), parts along dimension 0, may hold values from -6 to 6
- grad_out: bfloat16 [128, 256, 180], P(('grp', 'row'), 'col'), parts along dimension 0, may hold values from -8 to 8
- regions: int32 [128, 256], P(('grp', 'row'), 'col'), parts along dimension 0, may hold values from 0 to 15, as said below
- ln_gain: float32 [180], replicated, may hold values from 0.1 to 1.9
- ln_offset: float32 [180], replicated, may hold values from -1.5 to 1.5
- qkv_weight: bfloat16 [180, 540], replicated, may hold values from -0.4375 to 0.4375
- qkv_bias: float32 [540], replicated, may hold values from -1.5 to 1.5
- proj_weight: bfloat16 [180, 180], replicated, may hold values from -0.4375 to 0.4375
- bias_table: float32 [225, 6], replicated, may hold values from -4 to 320
Outputs:
- d_tokens: bfloat16 [128, 256, 180], P(('grp', 'row'), 'col'), parts along dimension 0
- d_qkv_weight: float32 [360, 540], P('grp'), parts along dimension 0
- d_qkv_bias: float32 [1080], P('grp'), parts along dimension 0
- d_proj_weight: float32 [360, 180], P('grp'), parts along dimension 0
- d_bias_table: float32 [450, 6], P('grp'), parts along dimension 0
- d_ln_gain: float32 [360], P('grp'), parts along dimension 0
- d_ln_offset: float32 [360], P('grp'), parts along dimension 0
There are 2 independent parts, one for each index of `grp`. A program takes and returns all parts, laid end to end along the dimension named above; an argument that names none is the same for every part. Nothing has to cross between parts.
Inputs may be any that keep to these rules, and one draw needn't show every extreme that they name: `regions`: A token attends only to tokens of its window with the same id. The map is a grid: the id is 4 a + b, where a, from 0 to 3, depends only on the token's row and b, from 0 to 3, only on its column.
All inputs are finite; a program needn't handle non-finite values.
Results may differ from a plain program's by a relative error of at most 0.0085.
Values may be sent and summed in bfloat16 or wider, within the bound.
A program may use at most 64 MiB of HBM per device.

v0:
```python
import jax
import jax.numpy as jnp
from jax import lax
from jax.sharding import PartitionSpec as P

HEADS = 6
WIN = 8
SHIFT = 4
masked_score = -10000.0


def from_behind(shard, axis, by):
    count = lax.axis_size(axis)
    return lax.ppermute(shard, axis, [(i, (i + by) % count) for i in range(count)])


def multiply(form, left, right):
    return jnp.einsum(form, left, right, preferred_element_type=jnp.float32)


def relative_onehot(table_rows):
    span_size = WIN * WIN
    position = jnp.arange(span_size, dtype=jnp.int32)
    row_pos = position // WIN
    col_pos = position % WIN
    entry_index = (
        (row_pos[:, None] - row_pos[None, :] + WIN - 1) * (2 * WIN - 1)
        + col_pos[:, None]
        - col_pos[None, :]
        + WIN
        - 1
    )
    return (
        entry_index.reshape(-1)[:, None] == jnp.arange(table_rows, dtype=jnp.int32)[None, :]
    ).astype(jnp.float32)


def normalize(values, gain_vec, offset_vec):
    as_float = values.astype(jnp.float32)
    center = jnp.mean(as_float, -1, keepdims=True)
    variance = jnp.mean(jnp.square(as_float - center), -1, keepdims=True)
    inv_std = lax.rsqrt(variance + 1e-05)
    unit_tokens = (as_float - center) * inv_std
    normed = (unit_tokens * gain_vec + offset_vec).astype(jnp.bfloat16)
    return (normed, unit_tokens, inv_std)


def project(normed, weights, offsets):
    channels = normed.shape[-1]
    summed = multiply("rcd,df->rcf", normed, weights) + offsets
    factor = jnp.where(jnp.arange(3 * channels) < channels, (channels // HEADS) ** (-0.5), 1.0)
    return (summed * factor).astype(jnp.bfloat16)


def window_band(qkv, grad_band, label_band, rel_bias, proj_weight):
    channels = grad_band.shape[-1]
    head_count = rel_bias.shape[0]
    head_size = channels // head_count
    tile_cols = grad_band.shape[1]
    win_count = tile_cols // WIN
    span_size = WIN * WIN

    def windows(array):
        array = array.reshape((WIN, win_count, WIN) + array.shape[2:])
        array = jnp.moveaxis(array, 1, 0)
        return array.reshape((win_count, span_size) + array.shape[3:])

    parted = windows(qkv).reshape(win_count, span_size, 3, head_count, head_size)
    query_part = parted[:, :, 0]
    key_part = parted[:, :, 1]
    value_part = parted[:, :, 2]
    grad_win = windows(grad_band)
    label_win = windows(label_band)
    matched = label_win[:, :, None] == label_win[:, None, :]
    scores = multiply("nihd,njhd->nhij", query_part, key_part) + rel_bias[None]
    scores = jnp.where(matched[:, None], scores, masked_score)
    probability = jax.nn.softmax(scores, axis=-1)
    prob_low = probability.astype(jnp.bfloat16)
    attended = (
        multiply("nhij,njhd->nihd", prob_low, value_part)
        .astype(jnp.bfloat16)
        .reshape(win_count * span_size, channels)
    )
    flat_grad = grad_win.reshape(win_count * span_size, channels)
    d_proj = multiply("tc,td->cd", attended, flat_grad)
    d_attended = (
        multiply("td,cd->tc", flat_grad, proj_weight)
        .astype(jnp.bfloat16)
        .reshape(win_count, span_size, head_count, head_size)
    )
    d_prob = multiply("nihd,njhd->nhij", d_attended, value_part)
    d_scores = probability * (d_prob - jnp.sum(probability * d_prob, -1, keepdims=True))
    score_sum = jnp.sum(d_scores, 0)
    d_score_low = d_scores.astype(jnp.bfloat16)
    d_query = multiply("nhij,njhd->nihd", d_score_low, key_part) * head_size ** (-0.5)
    d_key = multiply("nhij,nihd->njhd", d_score_low, query_part)
    d_value = multiply("nhij,nihd->njhd", prob_low, d_attended)
    d_qkv = (
        jnp.stack([d_query, d_key, d_value], 2)
        .astype(jnp.bfloat16)
        .reshape(win_count, span_size, 3 * channels)
    )
    array = d_qkv
    array = array.reshape((win_count, WIN, WIN) + array.shape[2:])
    array = jnp.moveaxis(array, 0, 1)
    return (array.reshape((WIN, tile_cols) + array.shape[3:]), d_proj, score_sum)


def attention_backward(qkv, grad_tile, label_tile, rel_bias, proj_weight):
    tile_rows = grad_tile.shape[0]
    band_count = tile_rows // WIN
    channels = grad_tile.shape[-1]
    head_count = rel_bias.shape[0]

    def to_bands(array):
        return array.reshape((band_count, WIN) + array.shape[1:])

    def band_step(running, pieces):
        d_qkv, d_proj, score_sum = window_band(
            pieces[0], pieces[1], pieces[2], rel_bias, proj_weight
        )
        return ((running[0] + d_proj, running[1] + score_sum), d_qkv)

    initial = (
        jnp.zeros((channels, channels), jnp.float32),
        jnp.zeros((head_count, WIN * WIN, WIN * WIN), jnp.float32),
    )
    totals, d_qkv = lax.scan(
        band_step, initial, (to_bands(qkv), to_bands(grad_tile), to_bands(label_tile))
    )
    return (d_qkv.reshape((tile_rows,) + d_qkv.shape[2:]), totals[0], totals[1])


def input_backward(d_qkv, normed, unit_tokens, inv_std, gain_vec, qkv_weight):
    d_weight = multiply("rcd,rcf->df", normed, d_qkv)
    d_offsets = jnp.sum(d_qkv.astype(jnp.float32), (0, 1))
    d_normed = multiply("rcf,df->rcd", d_qkv, qkv_weight)
    d_gain = jnp.sum(d_normed * unit_tokens, (0, 1))
    d_offset = jnp.sum(d_normed, (0, 1))
    scaled_grad = d_normed * gain_vec
    d_input = inv_std * (
        scaled_grad
        - jnp.mean(scaled_grad, -1, keepdims=True)
        - unit_tokens * jnp.mean(scaled_grad * unit_tokens, -1, keepdims=True)
    )
    return (d_input, d_weight, d_offsets, d_gain, d_offset)


def into_frame(member_one, member_two, member_three):
    below_one, below_two, below_three = from_behind(
        (member_one[:SHIFT], member_two[:SHIFT], member_three[:SHIFT]), "row", -1
    )
    member_one = jnp.concatenate([member_one[SHIFT:], below_one], 0)
    member_two = jnp.concatenate([member_two[SHIFT:], below_two], 0)
    member_three = jnp.concatenate([member_three[SHIFT:], below_three], 0)
    right_one, right_two, right_three = from_behind(
        (member_one[:, :SHIFT], member_two[:, :SHIFT], member_three[:, :SHIFT]), "col", -1
    )
    member_one = jnp.concatenate([member_one[:, SHIFT:], right_one], 1)
    member_two = jnp.concatenate([member_two[:, SHIFT:], right_two], 1)
    member_three = jnp.concatenate([member_three[:, SHIFT:], right_three], 1)
    return (member_one, member_two, member_three)


def back_proj(field):
    from_left = from_behind(field[:, -SHIFT:], "col", 1)
    field = jnp.concatenate([from_left, field[:, :-SHIFT]], 1)
    from_above = from_behind(field[-SHIFT:], "row", 1)
    return jnp.concatenate([from_above, field[:-SHIFT]], 0)


def table_grad(score_sum, entry_table):
    head_count = score_sum.shape[0]
    flat_sum = jnp.transpose(score_sum, (1, 2, 0)).reshape(-1, head_count)
    return jnp.dot(entry_table.T, flat_sum, precision=lax.Precision.HIGHEST)


def attention_sums(d_proj, d_table):
    return (d_proj, d_table)


def on_device(
    tokens, grad_out, regions, ln_gain, ln_offset, qkv_weight, qkv_bias, proj_weight, bias_table
):
    head_count = bias_table.shape[1]
    entry_table = relative_onehot(bias_table.shape[0])
    rel_bias = (
        jnp.dot(entry_table, bias_table, precision=lax.Precision.HIGHEST)
        .reshape(WIN * WIN, WIN * WIN, head_count)
        .transpose(2, 0, 1)
    )
    labels = regions.astype(jnp.bfloat16)
    normed, unit_tokens, inv_std = normalize(tokens, ln_gain, ln_offset)
    qkv = project(normed, qkv_weight, qkv_bias)
    qkv_framed, grad_framed, label_framed = into_frame(qkv, grad_out, labels)
    d_framed, d_proj, score_sum = attention_backward(
        qkv_framed, grad_framed, label_framed, rel_bias, proj_weight
    )
    d_proj, d_table = attention_sums(d_proj, table_grad(score_sum, entry_table))
    d_qkv = back_proj(d_framed)
    d_input, d_weight, d_offsets, d_gain, d_offset = input_backward(
        d_qkv, normed, unit_tokens, inv_std, ln_gain, qkv_weight
    )
    d_proj, d_table, d_weight, d_offsets, d_gain, d_offset = lax.psum(
        (d_proj, d_table, d_weight, d_offsets, d_gain, d_offset), ("row", "col")
    )
    total_tokens = tokens.shape[0] * tokens.shape[1] * lax.axis_size("row") * lax.axis_size("col")
    out_scale = total_tokens ** (-0.5)
    d_tokens = (grad_out.astype(jnp.float32) + d_input).astype(jnp.bfloat16)
    return (
        d_tokens,
        d_weight * out_scale,
        d_offsets * out_scale,
        d_proj * out_scale,
        d_table * out_scale,
        d_gain * out_scale,
        d_offset * out_scale,
    )


def solution(mesh):
    placed = (
        P(("grp", "row"), "col", None),
        P(("grp", "row"), "col", None),
        P(("grp", "row"), "col"),
        P(),
        P(),
        P(),
        P(),
        P(),
        P(),
    )
    return jax.shard_map(
        on_device,
        mesh=mesh,
        in_specs=placed,
        out_specs=(
            P(("grp", "row"), "col", None),
            P("grp", None),
            P("grp"),
            P("grp", None),
            P("grp", None),
            P("grp"),
            P("grp"),
        ),
        check_vma=False,
    )
```

profile of v0, /device:TPU:0, one launch (start us, length us, event | category | flops | bytes accessed | tf_op | source)
XLA Modules:
  0.0 272.9 jit_solution(3321277854407880220)
XLA Ops:
  7.2 1.1 convert_reduce_fusion.1
  8.3 1.1 fusion.40
  10.1 1.6 multiply_convert_fusion
  12.1 6.0 %collective-permute-start = (bf16[4,128,540]{1,0,2:T(4,128)(2,1)S(1)}, bf16[4,128,540]{1,0,2:T(4,128)(2,1)S(1)}, u32[]{:S(2)}, u32[]{:S(2)}) collective-permute-start(bf16[4,128,540]{1,0,2:T(4,128)(2,1)S(1)} %copy.87), channel_id=1, source_target_pairs={{0,14},{2,0},{4,2},{6,4},{8,6},{10,8},{12,10},{14,12},{1,15},{3,1}... | collective-permute-start | bytes 1658888 | tf_op jit(solution)/shard_map/ppermute | solution.py:14
  19.1 1.4 collective-permute-start.4
  20.7 0.6 copy-done.17
  21.3 2.6 fusion.2
  24.3 6.8 %collective-permute-done.2 = bf16[4,128]{1,0:T(4,128)(2,1)S(1)} collective-permute-done((bf16[4,128]{1,0:T(4,128)(2,1)S(1)}, bf16[4,128]{1,0:T(4,128)(2,1)S(1)}, u32[]{:S(2)}, u32[]{:S(2)}) %collective-permute-start.2) | collective-permute-done | bytes 1056 | tf_op jit(solution)/shard_map/ppermute | solution.py:14
  31.2 1.1 collective-permute-done.3
  32.9 2.7 %collective-permute-done.4 = bf16[4,128,180]{2,1,0:T(8,128)(2,1)S(1)} collective-permute-done((bf16[4,128,180]{2,1,0:T(8,128)(2,1)S(1)}, bf16[4,128,180]{2,1,0:T(8,128)(2,1)S(1)}, u32[]{:S(2)}, u32[]{:S(2)}) %collective-permute-start.4) | collective-permute-done | bytes 184352 | tf_op jit(solution)/shard_map/ppermute | solution.py:14
  35.8 1.0 collective-permute-done.5
  37.0 0.8 copy-done.2
  38.2 1.3 reshape.196
  40.7 0.7 collective-permute-done.1
  42.0 1.6 pad_maximum_fusion.3
  43.6 1.7 copy.91
  45.4 5.6 %reshape.191 = bf16[16,64,3,6,30]{4,3,2,1,0:T(8,128)(2,1)} reshape(bf16[16,8,8,540]{3,2,1,0:T(8,128)(2,1)S(1)} %copy.92) | data formatting | bytes 2211840 | tf_op jit(solution)/shard_map/while/body/eval_jaxpr/reshape;while/body/eval_jaxpr/reshape | solution.py:68
  51.1 6.6 %fusion.52 = (bf16[16,64,1,6,30]{4,3,2,1,0:T(8,128)(2,1)S(1)}, bf16[16,64,1,6,30]{4,3,2,1,0:T(8,128)(2,1)}, bf16[16,64,1,6,30]{4,3,2,1,0:T(8,128)(2,1)}) fusion(bf16[16,64,3,6,30]{4,3,2,1,0:T(8,128)(2,1)} %reshape.191), kind=kLoop, calls=%fused_computation.97 | loop fusion | bytes 2211840 | tf_op jit(solution)/shard_map/while/body/eval_jaxpr/slice | solution.py:71
  57.6 2.4 copy.123
  60.0 3.1 %copy.124 = bf16[16,64,1,6,30]{1,4,3,0,2:T(8,128)(2,1)} copy(bf16[16,64,1,6,30]{4,3,2,1,0:T(8,128)(2,1)} %get-tuple-element.77) | data formatting | bytes 737280
  63.2 1.9 copy.127
  65.1 1.7 fusion.26
  66.8 1.1 fusion.56
  68.2 1.0 multiply_reduce_fusion
  69.2 1.1 fusion.13
  71.4 0.9 fusion.9
  72.4 0.9 fusion.10
  73.3 0.6 pad_maximum_fusion
  73.9 5.5 %copy.108 = bf16[16,64,3,6,30]{4,3,2,1,0:T(8,128)(2,1)} copy(bf16[16,64,3,6,30]{1,4,3,0,2:T(8,128)(2,1)S(1)} %pad_maximum_fusion) | data formatting | bytes 2211840 | tf_op jit(solution)/shard_map/while/body/eval_jaxpr/stack | solution.py:99
  79.4 7.9 %convert_element_type.55 = bf16[16,8,8,540]{3,2,1,0:T(8,128)(2,1)} reshape(bf16[16,64,3,6,30]{4,3,2,1,0:T(8,128)(2,1)} %copy.108) | data formatting | bytes 2211840 | tf_op jit(solution)/shard_map/while/body/eval_jaxpr/convert_element_type | solution.py:100
  87.3 1.4 copy_bitcast_fusion
  89.0 0.8 copy.128
  91.0 1.1 copy.113
  92.8 1.5 fusion.11
  94.5 2.5 copy.116
  97.0 1.8 reshape.198
  98.8 1.4 fusion.1
  100.2 1.0 fusion.57
  101.2 9.2 %collective-permute-done.7 = bf16[4,128,540]{1,0,2:T(4,128)(2,1)} collective-permute-done((bf16[4,128,540]{1,0,2:T(4,128)(2,1)}, bf16[4,128,540]{1,0,2:T(4,128)(2,1)}, u32[]{:S(2)}, u32[]{:S(2)}) %collective-permute-start.7) | collective-permute-done | bytes 552992 | tf_op jit(solution)/shard_map/ppermute | solution.py:14
  110.4 1.1 copy.114
  112.6 0.7 fusion.39
  113.3 1.4 convolution_bitcast_fusion
  114.7 58.2 %all-reduce = (f32[540]{0:T(1024)S(1)}, f32[225,6]{0,1:T(8,128)S(1)}, f32[180]{0:T(256)S(1)}, f32[180]{0:T(256)S(1)}) all-reduce(f32[540]{0:T(1024)S(1)} %get-tuple-element.72, f32[225,6]{0,1:T(8,128)S(1)} %fusion.1, f32[180]{0:T(256)S(1)} %get-tuple-element.62, ...), channel_id=1, replica_groups=mesh['grp'=2,'row'=8,'col'=2] {'row','col'}, use_global_device_ids=true, to_apply=%region_9.10 | all-reduce | flops 2250 | bytes 18000 | tf_op jit(solution)/shard_map/psum | solution.py:204
  174.9 0.8 copy.118
  175.7 0.6 broadcast_multiply_fusion.2
  176.3 86.3 %all-reduce.4.cloned.1.call-done = (f32[180,540]{1,0:T(8,128)}, f32[180,180]{1,0:T(8,128)}) async-done(((f32[180,540]{1,0:T(8,128)}, f32[180,180]{1,0:T(8,128)}), (f32[180,540]{1,0:T(8,128)}, f32[180,180]{1,0:T(8,128)})) %all-reduce.4.cloned.1.call-update) | async-done | bytes 518416 | tf_op jit(solution)/shard_map/psum | solution.py:204
  262.6 1.8 broadcast_multiply_fusion
  264.5 1.6 broadcast_multiply_fusion.1
  (101 shorter events, 12.5 us)
Async XLA Ops:
  7.2 2.9 %copy-start = (bf16[180,540]{1,0:T(8,128)(2,1)S(1)}, bf16[180,540]{1,0:T(8,128)(2,1)}, u32[]{:S(2)}) copy-start(bf16[180,540]{1,0:T(8,128)(2,1)} %param.14) | copy-start | bytes 583204
  7.2 255.5 %all-reduce.4.cloned.1.call-start = ((), (), s32[]{:S(2)}) async-start(), calls=%async_computation | async-start | bytes 1318912 | tf_op jit(solution)/shard_map/psum | solution.py:204
  8.3 1.1 copy-start.13
  9.5 0.6 copy-start.15
  11.7 6.4 %copy-start.19 = (s32[8,128]{1,0:T(8,128)S(1)}, s32[8,128]{1,0:T(8,128)}, u32[]{:S(2)}) copy-start(s32[8,128]{1,0:T(8,128)} %param.11) | copy-start | bytes 12292
  11.7 7.0 %copy-start.7 = (bf16[8,128,180]{1,0,2:T(8,128)(2,1)S(1)}, bf16[8,128,180]{1,0,2:T(8,128)(2,1)}, u32[]{:S(2)}) copy-start(bf16[8,128,180]{1,0,2:T(8,128)(2,1)} %param.10) | copy-start | bytes 1105924
  11.7 9.5 %copy-start.21 = (f32[225,6]{0,1:T(8,128)S(1)}, f32[225,6]{0,1:T(8,128)}, u32[]{:S(2)}) copy-start(f32[225,6]{0,1:T(8,128)} %param.17) | copy-start | bytes 16204
  12.1 27.4 %collective-permute-start = (bf16[4,128,540]{1,0,2:T(4,128)(2,1)S(1)}, bf16[4,128,540]{1,0,2:T(4,128)(2,1)S(1)}, u32[]{:S(2)}, u32[]{:S(2)}) collective-permute-start(bf16[4,128,540]{1,0,2:T(4,128)(2,1)S(1)} %copy.87), channel_id=1, source_target_pairs={{0,14},{2,0},{4,2},{6,4},{8,6},{10,8},{12,10},{14,12},{1,15},{3,1}... | collective-permute-start | bytes 1658888 | tf_op jit(solution)/shard_map/ppermute | solution.py:14
  18.2 12.9 %collective-permute-start.2 = (bf16[4,128]{1,0:T(4,128)(2,1)S(1)}, bf16[4,128]{1,0:T(4,128)(2,1)S(1)}, u32[]{:S(2)}, u32[]{:S(2)}) collective-permute-start(bf16[4,128]{1,0:T(4,128)(2,1)S(1)} %get-tuple-element.84), channel_id=1, source_target_pairs={{0,14},{2,0},{4,2},{6,4},{8,6},{10,8},{12,10},{14,12},{1,15},{3,1}... | collective-permute-start | bytes 3080 | tf_op jit(solution)/shard_map/ppermute | solution.py:14
  19.1 16.5 %collective-permute-start.4 = (bf16[4,128,180]{2,1,0:T(8,128)(2,1)S(1)}, bf16[4,128,180]{2,1,0:T(8,128)(2,1)S(1)}, u32[]{:S(2)}, u32[]{:S(2)}) collective-permute-start(bf16[4,128,180]{2,1,0:T(8,128)(2,1)S(1)} %copy.126), channel_id=1, source_target_pairs={{0,14},{2,0},{4,2},{6,4},{8,6},{10,8},{12,10},{14,12},{1,15},{3,1}... | collective-permute-start | bytes 552968 | tf_op jit(solution)/shard_map/ppermute | solution.py:14
  20.7 0.6 copy-start.17
  24.1 13.8 %copy-start.12 = (bf16[180,180]{1,0:T(8,128)(2,1)S(1)}, bf16[180,180]{1,0:T(8,128)(2,1)}, u32[]{:S(2)}) copy-start(bf16[180,180]{1,0:T(8,128)(2,1)} %param.16) | copy-start | bytes 194404
  31.1 1.2 collective-permute-start.3
  35.6 1.2 collective-permute-start.5
  37.0 0.8 copy-start.2
  40.1 1.3 collective-permute-start.1
  66.8 1.1 copy-start.9
  66.8 1.3 copy-start.11
  67.9 4.4 %copy-start.5 = (f32[16,6,64,64]{2,3,1,0:T(8,128)}, f32[16,6,64,64]{2,3,1,0:T(8,128)S(1)}, u32[]{:S(2)}) copy-start(f32[16,6,64,64]{2,3,1,0:T(8,128)S(1)} %get-tuple-element.86) | copy-start | bytes 4718596
  70.3 1.1 copy-start.1
  88.8 1.3 collective-permute-start.6
  90.1 2.3 copy-start.10
  90.6 2.2 copy-start.6
  92.1 18.4 %collective-permute-start.7 = (bf16[4,128,540]{1,0,2:T(4,128)(2,1)}, bf16[4,128,540]{1,0,2:T(4,128)(2,1)}, u32[]{:S(2)}, u32[]{:S(2)}) collective-permute-start(bf16[4,128,540]{1,0,2:T(4,128)(2,1)} %copy.113), channel_id=1, source_target_pairs={{0,2},{2,4},{4,6},{6,8},{8,10},{10,12},{12,14},{14,0},{1,3},{3,5},... | collective-permute-start | bytes 1658888 | tf_op jit(solution)/shard_map/ppermute | solution.py:14
  94.3 4.5 %copy-start.18 = (s32[4096]{0:T(1024)S(1)}, s32[4096]{0:T(1024)}, u32[]{:S(2)}) copy-start(s32[4096]{0:T(1024)} %copy-done.17) | copy-start | bytes 49156
  94.4 5.8 %copy-start.3 = (bf16[16,8,8,180]{3,2,1,0:T(8,128)(2,1)S(1)}, bf16[16,8,8,180]{3,2,1,0:T(8,128)(2,1)}, u32[]{:S(2)}) copy-start(bf16[16,8,8,180]{3,2,1,0:T(8,128)(2,1)} %copy-done.2) | copy-start | bytes 1105924
  111.6 1.0 copy-start.4
  111.6 1.0 copy-start.14
  111.6 1.0 copy-start.16
  111.6 1.0 copy-start.20
  112.2 1.1 copy-start.22
  113.3 60.8 %copy-start.8 = (bf16[8,128,180]{1,0,2:T(8,128)(2,1)S(1)}, bf16[8,128,180]{1,0,2:T(8,128)(2,1)}, u32[]{:S(2)}) copy-start(bf16[8,128,180]{1,0,2:T(8,128)(2,1)} %param.10) | copy-start | bytes 1105924
Sparse Core Ops, SparseCore 0:
  174.2 88.4 all-reduce.3
where the time goes:
time: 274 us; the launch traced here: 273 us
  waiting for transfers between devices  108 us (39%)
  blocking collectives  58.2 us (21%)
  local copies, waits for them, and re-layouts  52.8 us (19%)
  matrix products  15.6 us (6%)
  other arithmetic  14.7 us (5%)
  between operations  14.5 us (5%)
  starting transfers between devices  8.96 us (3%)
    psum x1, waiting for transfers between devices, on_device(): lax.psum((d_proj, d_table, d_weight, d_offsets, d_gain, d_offset), ('row'...  86.3 us
    psum x1, blocking collectives, on_device(): lax.psum((d_proj, d_table, d_weight, d_offsets, d_gain, d_offset), ('row'...  58.2 us
    ppermute x8, waiting for transfers between devices, from_behind(): lax.ppermute(shard, axis, [(i, (i + by) % count) for i in range(count)])  21.8 us
    unnamed x53, local copies, waits for them, and re-layouts  13.1 us
    dot_general x11, matrix products, multiply(): return jnp.einsum(form, left, right, preferred_element_type=jnp.float32)  11.6 us
    ppermute x8, starting transfers between devices, from_behind(): lax.ppermute(shard, axis, [(i, (i + by) % count) for i in range(count)])  8.92 us
    convert_element_type x1, local copies, waits for them, and re-layouts, window_band(): d_qkv = jnp.stack([d_query, d_key, d_value], 2).astype(jnp.bfloat16).resh...  7.91 us
    slice x1, local copies, waits for them, and re-layouts, window_band(): value_part = parted[:, :, 2]  6.55 us
  transfers between devices with their start and end apart: 9, of which 8 were waited for; matrix products, arithmetic and copies ran while one was open for 7% of the time, Pallas kernels for 0%

commit v1 on v0

--- a/solution.py
+++ b/solution.py
@@ -202,7 +202,7 @@
         d_qkv, normed, unit_tokens, inv_std, ln_gain, qkv_weight
     )
     d_proj, d_table, d_weight, d_offsets, d_gain, d_offset = lax.psum(
-        (d_proj, d_table, d_weight, d_offsets, d_gain, d_offset), ("row", "col")
+        lax.psum((d_proj, d_table, d_weight, d_offsets, d_gain, d_offset), "col"), "row"
     )
     total_tokens = tokens.shape[0] * tokens.shape[1] * lax.axis_size("row") * lax.axis_size("col")
     out_scale = total_tokens ** (-0.5)

time: 274 us -> 236 us (0.86)
  blocking collectives: 58.2 us -> 37.9 us
  waiting for transfers between devices: 108 us -> 90.2 us
    psum x1 -> x2, blocking collectives: 58.2 us -> 37.9 us  [the longest x1 34.6 us: on_device(): lax.psum(lax.psum((d_proj, d_table, d_weight, d_offsets, d_gain, d_offset...]
    psum x1 -> x2, waiting for transfers between devices: 86.3 us -> 68.4 us  [the longest x1 68.4 us: on_device(): lax.psum(lax.psum((d_proj, d_table, d_weight, d_offsets, d_gain, d_offset...]
  transfers between devices with their start and end apart: 9 -> 10, of which waited for: 8 -> 8; matrix products, arithmetic and copies ran while one was open for 7% -> 8% of each run, Pallas kernels for 0% -> 0%
where the time goes in v1:
time: 236 us; the launch traced here: 235 us
  waiting for transfers between devices  90.2 us (38%)
  local copies, waits for them, and re-layouts  52.8 us (22%)
  blocking collectives  37.9 us (16%)
  matrix products  15.6 us (7%)
  other arithmetic  14.7 us (6%)
  between operations  14.5 us (6%)
  starting transfers between devices  9 us (4%)
    psum x1, waiting for transfers between devices, on_device(): lax.psum(lax.psum((d_proj, d_table, d_weight, d_offsets, d_gain, d_offset...  68.4 us
    psum x1, blocking collectives, on_device(): lax.psum(lax.psum((d_proj, d_table, d_weight, d_offsets, d_gain, d_offset...  34.6 us
    ppermute x8, waiting for transfers between devices, from_behind(): lax.ppermute(shard, axis, [(i, (i + by) % count) for i in range(count)])  21.8 us
    unnamed x53, local copies, waits for them, and re-layouts  13.1 us
    dot_general x11, matrix products, multiply(): return jnp.einsum(form, left, right, preferred_element_type=jnp.float32)  11.6 us
    ppermute x8, starting transfers between devices, from_behind(): lax.ppermute(shard, axis, [(i, (i + by) % count) for i in range(count)])  8.92 us
    convert_element_type x1, local copies, waits for them, and re-layouts, window_band(): d_qkv = jnp.stack([d_query, d_key, d_value], 2).astype(jnp.bfloat16).resh...  7.91 us
    slice x1, local copies, waits for them, and re-layouts, window_band(): value_part = parted[:, :, 2]  6.55 us
  transfers between devices with their start and end apart: 10, of which 8 were waited for; matrix products, arithmetic and copies ran while one was open for 8% of the time, Pallas kernels for 0%

profile of v1, /device:TPU:0, one launch (start us, length us, event | category | flops | bytes accessed | tf_op | source)
XLA Modules:
  0.0 234.7 jit_solution(12905361585052562238)
XLA Ops:
  7.2 1.1 convert_reduce_fusion.1
  8.3 1.1 fusion.40
  10.1 1.6 multiply_convert_fusion
  12.1 6.0 %collective-permute-start = (bf16[4,128,540]{1,0,2:T(4,128)(2,1)S(1)}, bf16[4,128,540]{1,0,2:T(4,128)(2,1)S(1)}, u32[]{:S(2)}, u32[]{:S(2)}) collective-permute-start(bf16[4,128,540]{1,0,2:T(4,128)(2,1)S(1)} %copy.87), channel_id=1, source_target_pairs={{0,14},{2,0},{4,2},{6,4},{8,6},{10,8},{12,10},{14,12},{1,15},{3,1}... | collective-permute-start | bytes 1658888 | tf_op jit(solution)/shard_map/ppermute | solution.py:14
  19.1 1.4 collective-permute-start.4
  20.7 0.6 copy-done.17
  21.3 2.6 %fusion.2 = f32[4096,6]{0,1:T(8,128)S(1)} fusion(f32[225,6]{0,1:T(8,128)S(1)} %copy-done.21, s32[4096]{0:T(1024)S(1)} %reshape.202), kind=kOutput, calls=%fused_computation.3 | convolution fusion | flops 67276800 | bytes 120088 | tf_op jit(solution)/shard_map/dot_general | solution.py:188
  24.3 6.8 %collective-permute-done.2 = bf16[4,128]{1,0:T(4,128)(2,1)S(1)} collective-permute-done((bf16[4,128]{1,0:T(4,128)(2,1)S(1)}, bf16[4,128]{1,0:T(4,128)(2,1)S(1)}, u32[]{:S(2)}, u32[]{:S(2)}) %collective-permute-start.2) | collective-permute-done | bytes 1056 | tf_op jit(solution)/shard_map/ppermute | solution.py:14
  31.2 1.1 collective-permute-done.3
  32.9 2.7 %collective-permute-done.4 = bf16[4,128,180]{2,1,0:T(8,128)(2,1)S(1)} collective-permute-done((bf16[4,128,180]{2,1,0:T(8,128)(2,1)S(1)}, bf16[4,128,180]{2,1,0:T(8,128)(2,1)S(1)}, u32[]{:S(2)}, u32[]{:S(2)}) %collective-permute-start.4) | collective-permute-done | bytes 184352 | tf_op jit(solution)/shard_map/ppermute | solution.py:14
  35.8 1.0 collective-permute-done.5
  37.0 0.8 copy-done.2
  38.2 1.3 reshape.196
  40.7 0.7 collective-permute-done.1
  42.0 1.6 pad_maximum_fusion.3
  43.6 1.7 copy.91
  45.4 5.6 %reshape.191 = bf16[16,64,3,6,30]{4,3,2,1,0:T(8,128)(2,1)} reshape(bf16[16,8,8,540]{3,2,1,0:T(8,128)(2,1)S(1)} %copy.92) | data formatting | bytes 2211840 | tf_op jit(solution)/shard_map/while/body/eval_jaxpr/reshape;while/body/eval_jaxpr/reshape | solution.py:68
  51.1 6.6 %fusion.52 = (bf16[16,64,1,6,30]{4,3,2,1,0:T(8,128)(2,1)S(1)}, bf16[16,64,1,6,30]{4,3,2,1,0:T(8,128)(2,1)}, bf16[16,64,1,6,30]{4,3,2,1,0:T(8,128)(2,1)}) fusion(bf16[16,64,3,6,30]{4,3,2,1,0:T(8,128)(2,1)} %reshape.191), kind=kLoop, calls=%fused_computation.97 | loop fusion | bytes 2211840 | tf_op jit(solution)/shard_map/while/body/eval_jaxpr/slice | solution.py:71
  57.6 2.4 %copy.123 = bf16[16,64,1,6,30]{1,4,3,0,2:T(8,128)(2,1)S(1)} copy(bf16[16,64,1,6,30]{4,3,2,1,0:T(8,128)(2,1)} %get-tuple-element.84) | data formatting | bytes 737280
  60.0 3.1 %copy.124 = bf16[16,64,1,6,30]{1,4,3,0,2:T(8,128)(2,1)} copy(bf16[16,64,1,6,30]{4,3,2,1,0:T(8,128)(2,1)} %get-tuple-element.83) | data formatting | bytes 737280
  63.2 1.9 copy.127
  65.1 1.7 fusion.26
  66.8 1.1 fusion.56
  68.2 1.0 multiply_reduce_fusion
  69.2 1.1 fusion.13
  71.4 0.9 fusion.9
  72.4 0.9 fusion.10
  73.3 0.6 pad_maximum_fusion
  73.9 5.5 %copy.108 = bf16[16,64,3,6,30]{4,3,2,1,0:T(8,128)(2,1)} copy(bf16[16,64,3,6,30]{1,4,3,0,2:T(8,128)(2,1)S(1)} %pad_maximum_fusion) | data formatting | bytes 2211840 | tf_op jit(solution)/shard_map/while/body/eval_jaxpr/stack | solution.py:99
  79.4 7.9 %convert_element_type.55 = bf16[16,8,8,540]{3,2,1,0:T(8,128)(2,1)} reshape(bf16[16,64,3,6,30]{4,3,2,1,0:T(8,128)(2,1)} %copy.108) | data formatting | bytes 2211840 | tf_op jit(solution)/shard_map/while/body/eval_jaxpr/convert_element_type | solution.py:100
  87.3 1.4 copy_bitcast_fusion
  89.0 0.8 copy.128
  91.0 1.1 copy.113
  92.8 1.5 fusion.11
  94.5 2.5 %copy.116 = bf16[16,64,6,30]{1,0,3,2:T(8,128)(2,1)} copy(bf16[16,64,6,30]{1,3,2,0:T(8,128)(2,1)} %fusion.11) | data formatting | bytes 737280 | tf_op jit(solution)/shard_map/while/body/eval_jaxpr/convert_element_type | solution.py:81
  97.0 1.8 reshape.198
  98.8 1.4 fusion.1
  100.2 1.0 fusion.57
  101.2 9.2 %collective-permute-done.7 = bf16[4,128,540]{1,0,2:T(4,128)(2,1)} collective-permute-done((bf16[4,128,540]{1,0,2:T(4,128)(2,1)}, bf16[4,128,540]{1,0,2:T(4,128)(2,1)}, u32[]{:S(2)}, u32[]{:S(2)}) %collective-permute-start.7) | collective-permute-done | bytes 552992 | tf_op jit(solution)/shard_map/ppermute | solution.py:14
  110.4 1.1 copy.114
  112.6 0.7 fusion.39
  113.3 1.4 convolution_bitcast_fusion
  114.8 3.3 %all-reduce.2 = (f32[540]{0:T(1024)S(1)}, f32[225,6]{0,1:T(8,128)S(1)}, f32[180]{0:T(256)S(1)}, f32[180]{0:T(256)S(1)}) all-reduce(f32[540]{0:T(1024)S(1)} %get-tuple-element.78, f32[225,6]{0,1:T(8,128)S(1)} %fusion.1, f32[180]{0:T(256)S(1)} %get-tuple-element.62, ...), channel_id=1, replica_groups=mesh['grp'=2,'row'=8,'col'=2] {'col'}, use_global_device_ids=true, to_apply=%region_10.11 | all-reduce | flops 2250 | bytes 18000 | tf_op jit(solution)/shard_map/psum | solution.py:205
  118.1 34.6 %all-reduce = (f32[540]{0:T(1024)S(1)}, f32[225,6]{0,1:T(8,128)S(1)}, f32[180]{0:T(256)S(1)}, f32[180]{0:T(256)S(1)}) all-reduce(f32[540]{0:T(1024)S(1)} %get-tuple-element.72, f32[225,6]{0,1:T(8,128)S(1)} %get-tuple-element.73, f32[180]{0:T(256)S(1)} %get-tuple-element.74, ...), channel_id=1, replica_groups=mesh['grp'=2,'row'=8,'col'=2] {'row'}, use_global_device_ids=true, to_apply=%region_11.12 | all-reduce | flops 2250 | bytes 18000 | tf_op jit(solution)/shard_map/psum | solution.py:204
  154.1 0.8 copy.118
  156.1 68.4 %all-reduce.7.cloned.1.call-done = (f32[180,540]{1,0:T(8,128)}, f32[180,180]{1,0:T(8,128)}) async-done(((f32[180,540]{1,0:T(8,128)}, f32[180,180]{1,0:T(8,128)}), (f32[180,540]{1,0:T(8,128)}, f32[180,180]{1,0:T(8,128)})) %all-reduce.7.cloned.1.call-update) | async-done | bytes 518416 | tf_op jit(solution)/shard_map/psum | solution.py:204
  224.5 1.8 broadcast_multiply_fusion
  226.3 1.6 broadcast_multiply_fusion.1
  (105 shorter events, 13.2 us)
Async XLA Ops:
  7.2 2.9 %copy-start = (bf16[180,540]{1,0:T(8,128)(2,1)S(1)}, bf16[180,540]{1,0:T(8,128)(2,1)}, u32[]{:S(2)}) copy-start(bf16[180,540]{1,0:T(8,128)(2,1)} %param.14) | copy-start | bytes 583204
  7.2 146.3 %all-reduce.9.cloned.1.call-start = ((), (), s32[]{:S(2)}) async-start(), calls=%async_computation.1 | async-start | bytes 1318912 | tf_op jit(solution)/shard_map/psum | solution.py:205
  8.3 1.1 copy-start.13
  9.5 0.6 copy-start.15
  11.7 6.4 %copy-start.19 = (s32[8,128]{1,0:T(8,128)S(1)}, s32[8,128]{1,0:T(8,128)}, u32[]{:S(2)}) copy-start(s32[8,128]{1,0:T(8,128)} %param.11) | copy-start | bytes 12292
  11.7 7.0 %copy-start.7 = (bf16[8,128,180]{1,0,2:T(8,128)(2,1)S(1)}, bf16[8,128,180]{1,0,2:T(8,128)(2,1)}, u32[]{:S(2)}) copy-start(bf16[8,128,180]{1,0,2:T(8,128)(2,1)} %param.10) | copy-start | bytes 1105924
  11.7 9.5 %copy-start.21 = (f32[225,6]{0,1:T(8,128)S(1)}, f32[225,6]{0,1:T(8,128)}, u32[]{:S(2)}) copy-start(f32[225,6]{0,1:T(8,128)} %param.17) | copy-start | bytes 16204
  12.1 27.4 %collective-permute-start = (bf16[4,128,540]{1,0,2:T(4,128)(2,1)S(1)}, bf16[4,128,540]{1,0,2:T(4,128)(2,1)S(1)}, u32[]{:S(2)}, u32[]{:S(2)}) collective-permute-start(bf16[4,128,540]{1,0,2:T(4,128)(2,1)S(1)} %copy.87), channel_id=1, source_target_pairs={{0,14},{2,0},{4,2},{6,4},{8,6},{10,8},{12,10},{14,12},{1,15},{3,1}... | collective-permute-start | bytes 1658888 | tf_op jit(solution)/shard_map/ppermute | solution.py:14
  18.2 12.9 %collective-permute-start.2 = (bf16[4,128]{1,0:T(4,128)(2,1)S(1)}, bf16[4,128]{1,0:T(4,128)(2,1)S(1)}, u32[]{:S(2)}, u32[]{:S(2)}) collective-permute-start(bf16[4,128]{1,0:T(4,128)(2,1)S(1)} %get-tuple-element.90), channel_id=1, source_target_pairs={{0,14},{2,0},{4,2},{6,4},{8,6},{10,8},{12,10},{14,12},{1,15},{3,1}... | collective-permute-start | bytes 3080 | tf_op jit(solution)/shard_map/ppermute | solution.py:14
  19.1 16.5 %collective-permute-start.4 = (bf16[4,128,180]{2,1,0:T(8,128)(2,1)S(1)}, bf16[4,128,180]{2,1,0:T(8,128)(2,1)S(1)}, u32[]{:S(2)}, u32[]{:S(2)}) collective-permute-start(bf16[4,128,180]{2,1,0:T(8,128)(2,1)S(1)} %copy.126), channel_id=1, source_target_pairs={{0,14},{2,0},{4,2},{6,4},{8,6},{10,8},{12,10},{14,12},{1,15},{3,1}... | collective-permute-start | bytes 552968 | tf_op jit(solution)/shard_map/ppermute | solution.py:14
  20.7 0.6 copy-start.17
  24.1 13.8 %copy-start.12 = (bf16[180,180]{1,0:T(8,128)(2,1)S(1)}, bf16[180,180]{1,0:T(8,128)(2,1)}, u32[]{:S(2)}) copy-start(bf16[180,180]{1,0:T(8,128)(2,1)} %param.16) | copy-start | bytes 194404
  31.1 1.2 collective-permute-start.3
  35.6 1.2 collective-permute-start.5
  37.0 0.8 copy-start.2
  40.1 1.3 collective-permute-start.1
  66.8 1.1 copy-start.9
  66.8 1.3 copy-start.11
  67.9 4.4 %copy-start.5 = (f32[16,6,64,64]{2,3,1,0:T(8,128)}, f32[16,6,64,64]{2,3,1,0:T(8,128)S(1)}, u32[]{:S(2)}) copy-start(f32[16,6,64,64]{2,3,1,0:T(8,128)S(1)} %get-tuple-element.92) | copy-start | bytes 4718596
  70.3 1.1 copy-start.1
  88.8 1.3 collective-permute-start.6
  90.1 2.3 copy-start.10
  90.6 2.2 copy-start.6
  92.1 18.4 %collective-permute-start.7 = (bf16[4,128,540]{1,0,2:T(4,128)(2,1)}, bf16[4,128,540]{1,0,2:T(4,128)(2,1)}, u32[]{:S(2)}, u32[]{:S(2)}) collective-permute-start(bf16[4,128,540]{1,0,2:T(4,128)(2,1)} %copy.113), channel_id=1, source_target_pairs={{0,2},{2,4},{4,6},{6,8},{8,10},{10,12},{12,14},{14,0},{1,3},{3,5},... | collective-permute-start | bytes 1658888 | tf_op jit(solution)/shard_map/ppermute | solution.py:14
  94.3 4.5 %copy-start.18 = (s32[4096]{0:T(1024)S(1)}, s32[4096]{0:T(1024)}, u32[]{:S(2)}) copy-start(s32[4096]{0:T(1024)} %copy-done.17) | copy-start | bytes 49156
  94.4 5.8 %copy-start.3 = (bf16[16,8,8,180]{3,2,1,0:T(8,128)(2,1)S(1)}, bf16[16,8,8,180]{3,2,1,0:T(8,128)(2,1)}, u32[]{:S(2)}) copy-start(bf16[16,8,8,180]{3,2,1,0:T(8,128)(2,1)} %copy-done.2) | copy-start | bytes 1105924
  111.6 1.0 copy-start.4
  111.6 1.0 copy-start.14
  111.6 1.0 copy-start.16
  111.6 1.0 copy-start.20
  112.2 1.1 copy-start.22
  113.3 39.9 %copy-start.8 = (bf16[8,128,180]{1,0,2:T(8,128)(2,1)S(1)}, bf16[8,128,180]{1,0,2:T(8,128)(2,1)}, u32[]{:S(2)}) copy-start(bf16[8,128,180]{1,0,2:T(8,128)(2,1)} %param.10) | copy-start | bytes 1105924
  114.7 109.7 %all-reduce.7.cloned.1.call-start = ((), (), s32[]{:S(2)}) async-start(), calls=%async_computation | async-start | bytes 1318912 | tf_op jit(solution)/shard_map/psum | solution.py:204
Sparse Core Ops, SparseCore 0:
  114.8 17.4 all-reduce.8
  153.7 70.7 all-reduce.6
